TPU v7x, 256 devices: a whole 4x4x8 slice. The times are simulated.
256 devices in a mesh: layer: 4 (over x), row: 64 (over y, z, core).
Axes of the slice: x: 4, y: 4, z: 8, core: 2. Of those that a mesh axis runs over, the one named last changes fastest.
Arguments:
- tokens: bfloat16 [128, 8192], P('row'), may hold values from -6 to 6
- up_weight: bfloat16 [4, 32768, 8192], P('layer', 'row'), may hold values from -6 to 6
- hess_panel: float32 [4, 256, 8192], P('layer', None, 'row'), may hold values from -1 to 2, as said below
- keep_mask: int32 [4, 32768, 256], P('layer', 'row'), may hold values from 0 to 1, as said below
Outputs:
- section_acts: bfloat16 [4, 128, 8192], P('layer', 'row')
- pruned_blocks: bfloat16 [4, 32768, 256], P('layer', 'row')
Inputs may be any that keep to these rules, and one draw needn't show every extreme that they name: `keep_mask`: each row has exactly 64 ones in each block of 128 columns. `hess_panel`: zero where the column is below the row; the diagonal lies in [0.5, 2].
All inputs are finite; a program needn't handle non-finite values.
Results may differ from a plain program's by a relative error of at most 0.017.
Values may be sent and summed in bfloat16 or wider, within the bound.
A program may use at most 192 MiB of HBM per device.

v0:
```python
import functools

import jax
import jax.numpy as jnp
from jax import lax
from jax.experimental import pallas as pl
from jax.experimental.pallas import tpu as pltpu
from jax.sharding import PartitionSpec as P

MESH = pl.DeviceIdType.MESH
BF16 = jnp.bfloat16
F32 = jnp.float32

BLOCK = 128
LEAD = 2 * BLOCK
DEPTH = 4
NY = 4
NZ = 8
LINE = 2 * NZ
FEATURES = 8192
UNITS = 512
TOKENS = 128
QUARTER = TOKENS // NY
PAIR = 2
epsilon = 1e-05

DOWN = 2.0**-32
UP = 2.0**32


def position():
    layer = lax.axis_index("layer")
    row = lax.axis_index("row")
    return layer, row // LINE, (row // 2) % NZ, row % 2


def device(layer, y, z, core):
    return (layer, (y * NZ + z) * 2 + core)


def meet(partners):
    barrier = pltpu.get_barrier_semaphore()
    for partner in partners:
        pl.semaphore_signal(barrier, inc=1, device_id=partner, device_id_type=MESH)
    pl.semaphore_wait(barrier, len(partners))


def remote(src, dst, send_sem, recv_sem, target):
    return pltpu.make_async_remote_copy(
        src_ref=src,
        dst_ref=dst,
        send_sem=send_sem,
        recv_sem=recv_sem,
        device_id=target,
        device_id_type=MESH,
    )


OFFSETS = [0, -1, 1, -2, 2, -3, 3, -4]


def offset_of(k):
    return jnp.where(k % 2 == 1, -((k + 1) // 2), k // 2)


def gather(here, block, line, sems, ready):
    layer, y, z, c = here
    zsend, zrecv, ysend, yrecv, csend, crecv = sems
    s = 1 - 2 * c
    other = 1 - c
    wrap_z = lambda v: (v + NZ) % NZ
    wrap_y = lambda v: (v + NY) % NY
    zf = device(layer, y, wrap_z(z + s), c)
    zb = device(layer, y, wrap_z(z - s), c)
    yf = device(layer, wrap_y(y + s), z, c)
    yb = device(layer, wrap_y(y - s), z, c)
    sibling = device(layer, y, z, other)
    y_from, y_to, y_far = wrap_y(y - s), wrap_y(y + s), wrap_y(y + 2)
    started = []

    def send(view, target, ssem, rsem):
        copy = remote(view, view, ssem, rsem, target)
        copy.start()
        started.append(copy)

    def arrive(view, source, ssem, rsem):
        remote(view, view, ssem, rsem, source).wait_recv()

    def along_y(k):
        view = block(y, wrap_z(z + s * OFFSETS[k]), c)
        send(view, yf, ysend.at[k], yrecv.at[k])
        send(view, yb, ysend.at[8 + k], yrecv.at[8 + k])

    def pass_on(k):
        view = block(y_from, wrap_z(z + s * OFFSETS[k]), c)
        arrive(view, yb, ysend.at[k], yrecv.at[k])
        send(view, yf, ysend.at[16 + k], yrecv.at[16 + k])

    own = block(y, z, c)
    send(own, zf, zsend.at[0], zrecv.at[0])
    send(own, zb, zsend.at[4], zrecv.at[4])
    along_y(0)
    for d in range(1, 5):
        view = block(y, wrap_z(z - s * d), c)
        arrive(view, zb, zsend.at[d - 1], zrecv.at[d - 1])
        if d < 4:
            send(view, zf, zsend.at[d], zrecv.at[d])
        along_y(2 * d - 1)
        if d < 4:
            view = block(y, wrap_z(z + s * d), c)
            arrive(view, zf, zsend.at[3 + d], zrecv.at[3 + d])
            if d < 3:
                send(view, zb, zsend.at[4 + d], zrecv.at[4 + d])
            along_y(2 * d)
        if d == 1:
            pass_on(0)
        else:
            pass_on(2 * d - 3)
            pass_on(2 * d - 2)
    send(line(y, c), sibling, csend.at[0], crecv.at[0])
    pass_on(7)
    send(line(y_from, c), sibling, csend.at[1], crecv.at[1])
    for k in range(8):
        arrive(block(y_to, wrap_z(z + s * OFFSETS[k]), c), yf, ysend.at[8 + k], yrecv.at[8 + k])
    send(line(y_to, c), sibling, csend.at[2], crecv.at[2])
    arrive(line(y, other), sibling, csend.at[0], crecv.at[0])
    arrive(line(y_to, other), sibling, csend.at[1], crecv.at[1])
    arrive(line(y_from, other), sibling, csend.at[2], crecv.at[2])

    def last(k, carry):
        zk = wrap_z(z + s * offset_of(k))
        view = block(y_far, zk, c)
        arrive(view, yb, ysend.at[16 + k], yrecv.at[16 + k])
        remote(view, view, csend.at[3 + k], crecv.at[3 + k], sibling).start()
        ready(zk, c)
        zo = wrap_z(z - s * offset_of(k))
        arrive(block(y_far, zo, other), sibling, csend.at[3 + k], crecv.at[3 + k])
        ready(zo, other)
        return carry

    lax.fori_loop(0, 8, last, 0)

    def last_sent(k, carry):
        view = block(y_far, wrap_z(z + s * offset_of(k)), c)
        remote(view, view, csend.at[3 + k], crecv.at[3 + k], sibling).wait_send()
        return carry

    lax.fori_loop(0, 8, last_sent, 0)
    for copy in started:
        copy.wait_send()


GATHER_SEMS = [
    pltpu.SemaphoreType.DMA((7,)),
    pltpu.SemaphoreType.DMA((7,)),
    pltpu.SemaphoreType.DMA((24,)),
    pltpu.SemaphoreType.DMA((24,)),
    pltpu.SemaphoreType.DMA((11,)),
    pltpu.SemaphoreType.DMA((11,)),
]


def ring_partners(here):
    layer, y, z, c = here
    return [
        device(layer, y, (z + 1) % NZ, c),
        device(layer, y, (z + NZ - 1) % NZ, c),
        device(layer, (y + 1) % NY, z, c),
        device(layer, (y + NY - 1) % NY, z, c),
        device(layer, y, z, 1 - c),
    ]


def panel_kernel(panel_ref, full_ref, *sems):
    here = position()
    _, y, z, c = here
    meet(ring_partners(here))
    full_ref[y * NZ + z, c] = panel_ref[...].astype(BF16)
    gather(
        here,
        lambda yy, zz, cc: full_ref.at[yy * NZ + zz, cc],
        lambda yy, cc: full_ref.at[pl.ds(yy * NZ, NZ), cc],
        sems,
        lambda zz, cc: None,
    )


def gather_panel(panel):
    rows, columns = panel.shape
    return pl.pallas_call(
        panel_kernel,
        out_shape=jax.ShapeDtypeStruct((NY * NZ, 2, rows, columns), BF16),
        in_specs=[pl.BlockSpec(memory_space=pltpu.VMEM)],
        out_specs=pl.BlockSpec(memory_space=pltpu.VMEM),
        scratch_shapes=GATHER_SEMS,
        compiler_params=pltpu.CompilerParams(
            collective_id=0, has_side_effects=True, vmem_limit_bytes=24 * 2**20
        ),
        name="gather_panel",
    )(panel)


SUB = 16


def eliminate_kernel(weight_ref, mask_ref, factor_ref, pruned_ref, errors_ref, scaled_ref):
    work = weight_ref[...].astype(F32).T
    first, second = factor_ref[0, 0].astype(F32), factor_ref[0, 1].astype(F32)
    eye = (
        lax.broadcasted_iota(jnp.int32, (BLOCK, BLOCK), 0)
        == lax.broadcasted_iota(jnp.int32, (BLOCK, BLOCK), 1)
    )
    diagonal = jnp.concatenate(
        [
            jnp.sum(jnp.where(eye, first[:BLOCK], 0.0), axis=1, keepdims=True),
            jnp.sum(jnp.where(eye, second[BLOCK:], 0.0), axis=1, keepdims=True),
        ],
        0,
    )
    dropped = 1.0 - mask_ref[...].astype(F32).T
    scaled_ref[...] = dropped * (1.0 / diagonal)
    turned = jnp.concatenate([first.T, second.T], 0)
    turned16 = turned.astype(BF16)
    count = LEAD // SUB
    finished = []
    high, low = [], []
    window = work[: 2 * SUB]
    for g in range(count):
        start = g * SUB
        final = g + 1 == count
        rows = SUB if final else 2 * SUB
        current = window[:rows]
        following = None
        if g + 2 < count:
            following = work[start + 2 * SUB : start + 3 * SUB]
            if g > 0:
                part = turned16[start + 2 * SUB : start + 3 * SUB, :start]
                following = (
                    following
                    - jnp.dot(part, jnp.concatenate(high, 0), preferred_element_type=F32)
                    - jnp.dot(part, jnp.concatenate(low, 0), preferred_element_type=F32)
                )
        local = []
        for o in range(SUB):
            j = start + o
            error = current[o : o + 1] * scaled_ref[j : j + 1, :]
            current = current - turned[start : start + rows, j : j + 1] * error
            local.append(error)
        errors = jnp.concatenate(local, 0)
        errors_high = errors.astype(BF16)
        errors_low = (errors - errors_high.astype(F32)).astype(BF16)
        high.append(errors_high)
        low.append(errors_low)
        finished.append(current[:SUB])
        if not final:
            window = current[SUB:]
            if following is not None:
                part = turned16[start + 2 * SUB : start + 3 * SUB, start : start + SUB]
                following = (
                    following
                    - jnp.dot(part, errors_high, preferred_element_type=F32)
                    - jnp.dot(part, errors_low, preferred_element_type=F32)
                )
                window = jnp.concatenate([window, following], 0)
    pruned_ref[...] = jnp.concatenate(finished, 0).T.astype(BF16)
    errors_ref[0] = jnp.concatenate(high, 0)
    errors_ref[1] = jnp.concatenate(low, 0)


def eliminate(weight, mask, factor):
    return pl.pallas_call(
        eliminate_kernel,
        grid=(1,),
        out_shape=(
            jax.ShapeDtypeStruct((UNITS, LEAD), BF16),
            jax.ShapeDtypeStruct((2, LEAD, UNITS), BF16),
        ),
        in_specs=[
            pl.BlockSpec((UNITS, LEAD), lambda i: (0, 0)),
            pl.BlockSpec((UNITS, LEAD), lambda i: (0, 0)),
            pl.BlockSpec((1, 2, LEAD, BLOCK), lambda i: (0, 0, 0, 0)),
        ],
        out_specs=(
            pl.BlockSpec((UNITS, LEAD), lambda i: (0, 0)),
            pl.BlockSpec((2, LEAD, UNITS), lambda i: (0, 0, 0)),
        ),
        scratch_shapes=[pltpu.VMEM((LEAD, UNITS), F32)],
        compiler_params=pltpu.CompilerParams(vmem_limit_bytes=32 * 2**20),
        name="eliminate",
    )(weight, mask, factor)


def exchange_line(here, pieces, landed, send_sems, recv_sems):
    layer, y, z, c = here
    me = 2 * z + c

    def message(i):
        peer = (me + i) % LINE
        return remote(
            pieces.at[peer],
            landed.at[me],
            send_sems.at[i],
            recv_sems.at[i],
            device(layer, y, peer // 2, peer % 2),
        )

    def start(i, carry):
        message(i).start()
        return carry

    def wait(i, carry):
        source = (me + LINE - i) % LINE
        remote(
            pieces.at[source],
            landed.at[source],
            send_sems.at[i],
            recv_sems.at[i],
            device(layer, y, source // 2, source % 2),
        ).wait_recv()
        message(i).wait_send()
        return carry

    lax.fori_loop(1, LINE, start, 0)
    landed[me] = pieces[me]
    lax.fori_loop(1, LINE, wait, 0)


def silu(v):
    return v / (1.0 + jnp.exp(-v))


def forward_kernel(
    tokens_ref,
    weight_ref,
    pruned_ref,
    errors_ref,
    panel_ref,
    acts_ref,
    x_ref,
    w_ref,
    u_ref,
    total_ref,
    squares_ref,
    scale_ref,
    out_ref,
    spread_ref,
    hand_ref,
    hold_ref,
    pieces_ref,
    landed_ref,
    pieces2_ref,
    landed2_ref,
    load_sems,
    token_send,
    token_recv,
    act_send,
    act_recv,
    spread_send,
    spread_recv,
    hand_send,
    hand_recv,
    *sems,
):
    here = position()
    layer, y, z, c = here
    me = 2 * z + c
    width = FEATURES // LINE

    loads = [
        pltpu.make_async_copy(pruned_ref, w_ref.at[0, :, pl.ds(0, LEAD)], load_sems.at[0]),
        pltpu.make_async_copy(
            weight_ref.at[:, pl.ds(LEAD, width - LEAD)],
            w_ref.at[0, :, pl.ds(LEAD, width - LEAD)],
            load_sems.at[1],
        ),
        pltpu.make_async_copy(panel_ref, u_ref, load_sems.at[2]),
    ]
    for k in range(1, LINE):
        loads.append(
            pltpu.make_async_copy(
                weight_ref.at[:, pl.ds(k * width, width)], w_ref.at[k], load_sems.at[2 + k]
            )
        )
    for load in loads:
        load.start()

    partners = [device(layer, y, ((me + i) % LINE) // 2, (me + i) % 2) for i in range(1, LINE)]
    partners += [device(layer, (y + i) % NY, z, c) for i in range(1, NY)]
    partners += [device((layer + i) % DEPTH, y, z, c) for i in (1, DEPTH - 1)]
    meet(partners)

    def block(yy, zz, cc):
        return x_ref.at[zz, cc, pl.ds(pl.multiple_of(yy * QUARTER, QUARTER), QUARTER), :]

    def hand_on(target):
        return remote(hand_ref, block(y, z, c), hand_send, hand_recv, target)

    @pl.when(layer == 0)
    def _():
        tokens = tokens_ref[...].astype(F32)
        for p in range(LINE):
            for b in range(4):
                at = p * width + b * 128
                pieces_ref[p, PAIR * b : PAIR * (b + 1), :] = tokens[:, at : at + 128]
        exchange_line(here, pieces_ref, landed_ref, token_send, token_recv)
        for p in range(LINE):
            for b in range(4):
                hold_ref[PAIR * p : PAIR * (p + 1), b * 128 : (b + 1) * 128] = landed_ref[
                    p, PAIR * b : PAIR * (b + 1), :
                ]
        x_ref[z, c, pl.ds(pl.multiple_of(y * QUARTER, QUARTER), QUARTER), :] = hold_ref[...].astype(BF16)

    @pl.when(layer > 0)
    def _():
        hand_on(device((layer + DEPTH - 1) % DEPTH, y, z, c)).wait_recv()

    total_ref[...] = jnp.zeros_like(total_ref)
    squares_ref[...] = jnp.zeros_like(squares_ref)
    for load in loads:
        load.wait()
    u_ref[0] = jnp.zeros_like(u_ref[0])

    def ready(zz, cc):
        k = 2 * zz + cc
        x = x_ref[zz, cc]
        product = lax.dot_general(x, w_ref[k], (((1,), (1,)), ((), ())), preferred_element_type=F32)
        factor = jnp.concatenate(
            [u_ref[2 * k, 0], u_ref[2 * k, 1], u_ref[2 * k + 1, 0], u_ref[2 * k + 1, 1]], 1
        )
        inputs = lax.dot_general(x, factor, (((1,), (1,)), ((), ())), preferred_element_type=F32)
        total_ref[:, :UNITS] += product
        total_ref[:, UNITS:] += inputs
        wide = x.astype(F32)
        wide = wide * wide
        squares_ref[...] += wide[:, :128] + wide[:, 128:256] + wide[:, 256:384] + wide[:, 384:]

    gather(
        here,
        block,
        lambda yy, cc: x_ref.at[:, cc, pl.ds(pl.multiple_of(yy * QUARTER, QUARTER), QUARTER), :],
        sems,
        ready,
    )

    moment = jnp.sum(squares_ref[...], axis=1, keepdims=True) * (UP * UP / FEATURES)
    scale = jnp.where(layer == 0, 1.0, lax.rsqrt(moment + epsilon) * UP)
    scale_ref[...] = jnp.broadcast_to(scale, scale_ref.shape)
    inputs = total_ref[:, UNITS:]
    inputs_high = inputs.astype(BF16)
    inputs_low = (inputs - inputs_high.astype(F32)).astype(BF16)
    correction = (
        jnp.dot(inputs_high, errors_ref[0], preferred_element_type=F32)
        + jnp.dot(inputs_low, errors_ref[0], preferred_element_type=F32)
        + jnp.dot(inputs_high, errors_ref[1], preferred_element_type=F32)
    )
    output = ((total_ref[:, :UNITS] - correction) * (scale * FEATURES**-0.5)).astype(BF16)
    for q in range(NY):
        out_ref[q] = output[q * QUARTER : (q + 1) * QUARTER]

    spreads = []
    for i in range(1, NY):
        q = (y + i) % NY
        copy = remote(
            out_ref.at[q], spread_ref.at[y], spread_send.at[i], spread_recv.at[i], device(layer, q, z, c)
        )
        copy.start()
        spreads.append(copy)
    spread_ref[y] = out_ref[y]
    rows = pl.ds(pl.multiple_of(y * QUARTER, QUARTER), QUARTER)
    residual = x_ref[z, c, rows, :].astype(F32) * scale_ref[rows, :1]
    for i in range(1, NY):
        q = (y + NY - i) % NY
        remote(
            out_ref.at[q], spread_ref.at[q], spread_send.at[i], spread_recv.at[i], device(layer, q, z, c)
        ).wait_recv()
    folded = (
        silu(spread_ref[0].astype(F32))
        + silu(spread_ref[1].astype(F32))
        + silu(spread_ref[2].astype(F32))
        + silu(spread_ref[3].astype(F32))
    )
    combined = residual + folded
    following = device((layer + 1) % DEPTH, y, z, c)

    @pl.when(layer < DEPTH - 1)
    def _():
        hand_ref[...] = (combined * DOWN).astype(BF16)
        hand_on(following).start()

    for p in range(LINE):
        for b in range(4):
            pieces2_ref[p, PAIR * b : PAIR * (b + 1), :] = combined[
                PAIR * p : PAIR * (p + 1), b * 128 : (b + 1) * 128
            ]
    exchange_line(here, pieces2_ref, landed2_ref, act_send, act_recv)
    pair = landed2_ref[...]
    sums = jnp.sum(jnp.sum(pair * pair, axis=0), axis=1, keepdims=True)
    token = lax.broadcasted_iota(jnp.int32, (PAIR * 4, 1), 0) % PAIR
    mean0 = jnp.sum(jnp.where(token == 0, sums, 0.0), axis=0, keepdims=True) * (1.0 / FEATURES)
    mean1 = jnp.sum(jnp.where(token == 1, sums, 0.0), axis=0, keepdims=True) * (1.0 / FEATURES)
    normal = lax.rsqrt(jnp.where(token == 0, mean0, mean1) + epsilon)
    acts = (pair * normal[None]).astype(F32)
    for p in range(LINE):
        for b in range(4):
            at = p * width + b * 128
            acts_ref[:, at : at + 128] = acts[p, PAIR * b : PAIR * (b + 1), :].astype(BF16)

    for copy in spreads:
        copy.wait_send()

    @pl.when(layer < DEPTH - 1)
    def _():
        hand_on(following).wait_send()


def forward(tokens, weight, pruned, errors, panel):
    width = FEATURES // LINE
    vmem = pl.BlockSpec(memory_space=pltpu.VMEM)
    hbm = pl.BlockSpec(memory_space=pl.ANY)
    dma = pltpu.SemaphoreType.DMA
    return pl.pallas_call(
        forward_kernel,
        out_shape=jax.ShapeDtypeStruct((PAIR, FEATURES), BF16),
        in_specs=[vmem, hbm, hbm, vmem, hbm],
        out_specs=vmem,
        scratch_shapes=[
            pltpu.VMEM((NZ, 2, TOKENS, width), BF16),
            pltpu.VMEM((LINE, UNITS, width), BF16),
            pltpu.VMEM(panel.shape, BF16),
            pltpu.VMEM((TOKENS, UNITS + LEAD), F32),
            pltpu.VMEM((TOKENS, 128), F32),
            pltpu.VMEM((TOKENS, 128), F32),
            pltpu.VMEM((NY, QUARTER, UNITS), BF16),
            pltpu.VMEM((NY, QUARTER, UNITS), BF16),
            pltpu.VMEM((QUARTER, UNITS), BF16),
            pltpu.VMEM((QUARTER, UNITS), F32),
            pltpu.VMEM((LINE, PAIR * 4, 128), F32),
            pltpu.VMEM((LINE, PAIR * 4, 128), F32),
            pltpu.VMEM((LINE, PAIR * 4, 128), F32),
            pltpu.VMEM((LINE, PAIR * 4, 128), F32),
            dma((LINE + 2,)),
            dma((LINE,)),
            dma((LINE,)),
            dma((LINE,)),
            dma((LINE,)),
            dma((NY,)),
            dma((NY,)),
            dma,
            dma,
            *GATHER_SEMS,
        ],
        compiler_params=pltpu.CompilerParams(
            collective_id=1, has_side_effects=True, vmem_limit_bytes=48 * 2**20
        ),
        name="forward",
    )(tokens, weight, pruned, errors, panel)


def per_device(tokens, up_weight, hess_panel, keep_mask):
    weight = up_weight[0]
    panel = gather_panel(hess_panel[0])
    pruned, errors = eliminate(weight, keep_mask[0], panel)
    acts = forward(tokens, weight, pruned, errors, panel)
    return (acts[None], pruned[None])


def solution(mesh):
    in_specs = (
        P("row", None),
        P("layer", "row", None),
        P("layer", None, "row"),
        P("layer", "row", None),
    )
    out_specs = (P("layer", "row", None), P("layer", "row", None))
    return jax.shard_map(
        per_device, mesh=mesh, in_specs=in_specs, out_specs=out_specs, check_vma=False
    )
```

profile of v0, /device:TPU:7, one launch (start us, length us, event | category | flops | bytes accessed | tf_op | source)
XLA Modules:
  0.0 202.3 jit_solution(10390822962084617945)
XLA Ops:
  0.6 0.0 copy-start.3
  0.6 0.9 copy-done.3
  1.5 0.0 copy-start.4
  1.5 37.1 %gather_panel.1.factor_ref.panel_ref = bf16[32,2,256,128]{3,2,1,0:T(8,128)(2,1)S(1)} custom-call(f32[256,128]{1,0:T(8,128)S(1)} %bitcast.10), custom_call_target="tpu_custom_call" | custom-call | tf_op jit(solution)/shard_map/gather_panel/pallas_call | solution.py:190
  38.6 0.0 copy-start
  38.6 3.4 %copy-done = bf16[1,512,8192]{2,1,0:T(8,128)(2,1)S(1)} copy-done((bf16[1,512,8192]{2,1,0:T(8,128)(2,1)S(1)}, bf16[1,512,8192]{2,1,0:T(8,128)(2,1)}, u32[]{:S(2)}) %copy-start) | copy-done | bytes 8388632
  42.0 0.0 copy-start.1
  42.0 1.0 copy-done.1
  43.0 3.5 %eliminate.1 = (bf16[512,256]{1,0:T(8,128)(2,1)}, bf16[2,256,512]{2,1,0:T(8,128)(2,1)S(1)}) custom-call(bf16[512,8192]{1,0:T(8,128)(2,1)S(1)} %bitcast.6, s32[512,256]{1,0:T(8,128)S(1)} %bitcast.7, bf16[32,2,256,128]{3,2,1,0:T(8,128)(2,1)S(1)} %gather_panel.1.factor_ref.panel_ref), custom_call_target="tpu_custom_call" | custom-call | tf_op jit(solution)/shard_map/eliminate/pallas_call | solution.py:271
  46.5 0.0 copy-done.4
  46.5 0.0 copy-start.2
  46.5 0.9 copy-done.2
  47.5 154.2 %forward.1 = bf16[2,8192]{1,0:T(2,128)(2,1)S(1)} custom-call(bf16[2,8192]{1,0:T(2,128)(2,1)S(1)} %copy-done.4, bf16[512,8192]{1,0:T(8,128)(2,1)} %bitcast.5, bf16[512,256]{1,0:T(8,128)(2,1)S(1)} %copy-done.2, bf16[2,256,512]{2,1,0:T(8,128)(2,1)S(1)} %get-tuple-element.5.errors_ref, bf16[32,2,256,128]{3,2,1,0:T(8,128)(2,1)S(1)} %gather_panel.1.factor_ref.panel_ref), custom_call_target="tpu_custom_call" | custom-call | tf_op jit(solution)/shard_map/forward/pallas_call | solution.py:521
  201.7 0.6 copy.7
Async XLA Ops:
  0.6 0.9 copy-start.3
  1.5 45.0 %copy-start.4 = (bf16[2,8192]{1,0:T(2,128)(2,1)S(1)}, bf16[2,8192]{1,0:T(2,128)(2,1)}, u32[]{:S(2)}) copy-start(bf16[2,8192]{1,0:T(2,128)(2,1)} %tokens_ref.1) | copy-start | bytes 98308
  38.6 3.4 %copy-start = (bf16[1,512,8192]{2,1,0:T(8,128)(2,1)S(1)}, bf16[1,512,8192]{2,1,0:T(8,128)(2,1)}, u32[]{:S(2)}) copy-start(bf16[1,512,8192]{2,1,0:T(8,128)(2,1)} %param.5) | copy-start | bytes 25165828
  42.0 1.0 copy-start.1
  46.5 1.0 copy-start.2
where the time goes:
time: 203 us; the launch traced here: 202 us
  Pallas kernels  195 us (96%)
  local copies, waits for them, and re-layouts  6.89 us (3%)
    pallas_call x1, Pallas kernels, forward(): pl.pallas_call(forward_kernel, out_shape=jax.ShapeDtypeStruct((PAIR, FEAT...  154 us
    pallas_call x1, Pallas kernels, gather_panel(): pl.pallas_call(panel_kernel, out_shape=jax.ShapeDtypeStruct((NY * NZ, 2,...  37.1 us
    unnamed x11, local copies, waits for them, and re-layouts  6.89 us

commit v1 on v0

v1 whole, which is shorter than its diff:
```python
import functools

import jax
import jax.numpy as jnp
from jax import lax
from jax.experimental import pallas as pl
from jax.experimental.pallas import tpu as pltpu
from jax.sharding import PartitionSpec as P

MESH = pl.DeviceIdType.MESH
TRANSPOSED = (((1,), (1,)), ((), ()))
BF16 = jnp.bfloat16
F32 = jnp.float32

BLOCK = 128
LEAD = 2 * BLOCK
DEPTH = 4
NY = 4
NZ = 8
LINE = 2 * NZ
FEATURES = 8192
UNITS = 512
TOKENS = 128
QUARTER = TOKENS // NY
PAIR = 2
epsilon = 1e-05

DOWN = 2.0**-32
UP = 2.0**32


def position():
    layer = lax.axis_index("layer")
    row = lax.axis_index("row")
    return layer, row // LINE, (row // 2) % NZ, row % 2


def device(layer, y, z, core):
    return (layer, (y * NZ + z) * 2 + core)


def meet(partners):
    barrier = pltpu.get_barrier_semaphore()
    for partner in partners:
        pl.semaphore_signal(barrier, inc=1, device_id=partner, device_id_type=MESH)
    pl.semaphore_wait(barrier, len(partners))


def remote(src, dst, send_sem, recv_sem, target):
    return pltpu.make_async_remote_copy(
        src_ref=src,
        dst_ref=dst,
        send_sem=send_sem,
        recv_sem=recv_sem,
        device_id=target,
        device_id_type=MESH,
    )


Z_SLOTS = 8
NEAR = slice(0, 5)
FAR = slice(5, 8)
Y_PLACES = 4
BACK = {1: 2, 2: 1, 3: 3}


def slot_z(z, k):
    s = 1 - 2 * (z % 2)
    return (z + NZ + [0, -1, 1, -2 * s, 2 * s, -3, 3, 4][k]) % NZ


def number(condition):
    return condition.astype(jnp.int32)


def z_slot(z, target):
    odd = z % 2
    d = (target - z + NZ) % NZ
    fixed = number(d == 7) + 2 * number(d == 1) + 5 * number(d == 5) + 6 * number(d == 3) + 7 * number(d == 4)
    return fixed + (4 - odd) * number(d == 2) + (3 + odd) * number(d == 6)


def y_place(y, target):
    d = (target - y + NY) % NY
    return d + number(d == 2) - number(d == 3)


class Gather:
    def __init__(self, here, view, sems):
        self.layer, self.y, self.z, self.c = here
        self.view = view
        self.send_sems, self.recv_sems = sems
        odd = self.z % 2
        self.on, self.two_on, self.back = 1 - 2 * odd, 2 - 4 * odd, 2 * odd - 1
        self.two = {2: 3 + odd, -2: 4 - odd}
        self.behind_in, self.ahead_in = 2 + odd, 3 - odd
        self.behind_slot, self.behind_out = 5 + odd, 4 + odd
        self.ahead_slot, self.ahead_out = 6 - odd, 5 - odd
        self.sent = {0: {}, 1: {}}

    def copy(self, core, src, dst, dy, dz, message):
        src, dst = (self.view(slots, core, places) for slots, places in (src, dst))
        target = device(self.layer, (self.y + dy + NY) % NY, (self.z + dz + NZ) % NZ, core)
        return remote(src, dst, self.send_sems.at[message], self.recv_sems.at[message], target)

    def send(self, core, src, dst, dy, dz, message, name=None):
        self.copy(core, src, dst, dy, dz, message).start()
        self.sent[core][name or message] = lambda: self.copy(core, src, dst, dy, dz, message).wait_send()

    def arrive(self, core, dst, message):
        self.copy(core, dst, dst, 1, 0, message).wait_recv()

    def z_out(self, core, places):
        own = (0, places)
        for dz, message in ((2, 2), (-2, 3)):
            self.send(core, own, (self.two[dz], places), 0, dz, message)
        self.send(core, own, (1, places), 0, 1, 0)
        self.send(core, own, (2, places), 0, -1, 1)

    def z_relay(self, core, places):
        behind, ahead = (3, places), (4, places)
        self.arrive(core, behind, self.behind_in)
        self.send(core, behind, (7, places), 0, self.two_on, 6)
        self.send(core, behind, (self.behind_slot, places), 0, self.on, self.behind_out, "behind")
        self.arrive(core, ahead, self.ahead_in)
        self.send(core, ahead, (self.ahead_slot, places), 0, self.back, self.ahead_out, "ahead")

    def z_in(self, core, places, slots):
        for slot in slots:
            self.arrive(core, (slot, places), {1: 0, 2: 1, 5: 4, 6: 5, 7: 6}[slot])

    def y_out(self, core, slots, message):
        own = (slots, 0)
        for place, dy in ((3, 2), (1, 1), (2, -1)):
            self.send(core, own, (slots, BACK[place]), dy, 0, message + place - 1)

    def y_in(self, core, slots, message):
        for place in (1, 2, 3):
            self.arrive(core, (slots, place), message + BACK[place] - 1)

    def other(self, core, slots, message):
        view = self.view(slots, core, slice(0, Y_PLACES))
        target = device(self.layer, self.y, self.z, 1 - self.c)
        return remote(view, view, self.send_sems.at[message], self.recv_sems.at[message], target)

    def to_other(self, core, slots, message):
        self.other(core, slots, message).start()
        self.sent[core][message] = lambda: self.other(core, slots, message).wait_send()

    def from_other(self, slots, message):
        self.other(1 - self.c, slots, message).wait_recv()

    def part(self, core, i):
        every = slice(0, Y_PLACES)
        if core == 0:
            if i == 0:
                self.z_out(core, 0)
                self.y_out(core, 0, 7)
            elif i == 1:
                self.z_relay(core, 0)
                self.z_in(core, 0, (1, 2))
                self.y_out(core, slice(1, 5), 10)
            elif i == 2:
                self.z_in(core, 0, (5, 6, 7))
                self.y_out(core, FAR, 13)
            elif i == 3:
                self.y_in(core, 0, 7)
                self.y_in(core, slice(1, 5), 10)
                self.to_other(core, NEAR, 16)
            else:
                self.y_in(core, FAR, 13)
                self.to_other(core, FAR, 17)
        else:
            if i == 0:
                self.y_out(core, 0, 7)
            elif i == 1:
                self.y_in(core, 0, 7)
                self.z_out(core, every)
            elif i == 2:
                self.z_relay(core, every)
            elif i == 3:
                self.z_in(core, every, (1, 2))
                self.to_other(core, NEAR, 16)
            else:
                self.z_in(core, every, (5, 6, 7))
                self.to_other(core, FAR, 17)

    def finish(self, core):
        for wait in self.sent[core].values():
            wait()


GATHER_SEMS = [pltpu.SemaphoreType.DMA((18,)), pltpu.SemaphoreType.DMA((18,))]


def by_core(c, part):
    for core in (0, 1):
        pl.when(c == core)(functools.partial(part, core))


SUB = 16


def eliminate(weight_ref, mask_ref, factor_ref, pruned_ref, errors_ref, scaled_ref):
    work = weight_ref[...].astype(F32).T
    first, second = factor_ref[0].astype(F32), factor_ref[1].astype(F32)
    eye = (
        lax.broadcasted_iota(jnp.int32, (BLOCK, BLOCK), 0)
        == lax.broadcasted_iota(jnp.int32, (BLOCK, BLOCK), 1)
    )
    diagonal = jnp.concatenate(
        [
            jnp.sum(jnp.where(eye, first[:BLOCK], 0.0), axis=1, keepdims=True),
            jnp.sum(jnp.where(eye, second[BLOCK:], 0.0), axis=1, keepdims=True),
        ],
        0,
    )
    dropped = 1.0 - mask_ref[...].astype(F32).T
    scaled_ref[...] = dropped * (1.0 / diagonal)
    turned = jnp.concatenate([first.T, second.T], 0)
    turned16 = turned.astype(BF16)
    count = LEAD // SUB
    finished = []
    high, low = [], []
    window = work[: 2 * SUB]
    for g in range(count):
        start = g * SUB
        final = g + 1 == count
        rows = SUB if final else 2 * SUB
        current = window[:rows]
        following = None
        if g + 2 < count:
            following = work[start + 2 * SUB : start + 3 * SUB]
            if g > 0:
                part = turned16[start + 2 * SUB : start + 3 * SUB, :start]
                following = (
                    following
                    - jnp.dot(part, jnp.concatenate(high, 0), preferred_element_type=F32)
                    - jnp.dot(part, jnp.concatenate(low, 0), preferred_element_type=F32)
                )
        local = []
        for o in range(SUB):
            j = start + o
            error = current[o : o + 1] * scaled_ref[j : j + 1, :]
            current = current - turned[start : start + rows, j : j + 1] * error
            local.append(error)
        errors = jnp.concatenate(local, 0)
        errors_high = errors.astype(BF16)
        errors_low = (errors - errors_high.astype(F32)).astype(BF16)
        high.append(errors_high)
        low.append(errors_low)
        finished.append(current[:SUB])
        if not final:
            window = current[SUB:]
            if following is not None:
                part = turned16[start + 2 * SUB : start + 3 * SUB, start : start + SUB]
                following = (
                    following
                    - jnp.dot(part, errors_high, preferred_element_type=F32)
                    - jnp.dot(part, errors_low, preferred_element_type=F32)
                )
                window = jnp.concatenate([window, following], 0)
    pruned_ref[...] = jnp.concatenate(finished, 0).T.astype(BF16)
    errors_ref[0] = jnp.concatenate(high, 0)
    errors_ref[1] = jnp.concatenate(low, 0)


def exchange_line(here, pieces, landed, send_sems, recv_sems):
    layer, y, z, c = here
    me = 2 * z + c

    def message(i):
        peer = (me + i) % LINE
        return remote(
            pieces.at[peer],
            landed.at[me],
            send_sems.at[i],
            recv_sems.at[i],
            device(layer, y, peer // 2, peer % 2),
        )

    def start(i, carry):
        message(i).start()
        return carry

    def wait(i, carry):
        source = (me + LINE - i) % LINE
        remote(
            pieces.at[source],
            landed.at[source],
            send_sems.at[i],
            recv_sems.at[i],
            device(layer, y, source // 2, source % 2),
        ).wait_recv()
        message(i).wait_send()
        return carry

    lax.fori_loop(1, LINE, start, 0)
    landed[me] = pieces[me]
    return lambda: lax.fori_loop(1, LINE, wait, 0)


def silu(v):
    return v / (1.0 + jnp.exp(-v))


def forward_kernel(
    tokens_hbm,
    weight_ref,
    panel_hbm,
    mask_hbm,
    acts_ref,
    pruned_ref,
    tokens_ref,
    panel_ref,
    mask_ref,
    leading_ref,
    lead_ref,
    scaled_ref,
    errors_ref,
    x_ref,
    w_ref,
    u_ref,
    total_ref,
    squares_ref,
    out_ref,
    spread_ref,
    hand_ref,
    pieces_ref,
    landed_ref,
    pieces2_ref,
    landed2_ref,
    load_sems,
    lead_send,
    lead_recv,
    token_send,
    token_recv,
    act_send,
    act_recv,
    spread_send,
    spread_recv,
    hand_send,
    hand_recv,
    *sems,
):
    here = position()
    layer, y, z, c = here
    me = 2 * z + c
    width = FEATURES // LINE

    loads = [
        pltpu.make_async_copy(panel_hbm, panel_ref, load_sems.at[0]),
        pltpu.make_async_copy(tokens_hbm, tokens_ref, load_sems.at[1]),
        pltpu.make_async_copy(mask_hbm, mask_ref, load_sems.at[2]),
        pltpu.make_async_copy(weight_ref.at[:, pl.ds(0, LEAD)], leading_ref, load_sems.at[3]),
        pltpu.make_async_copy(
            weight_ref.at[:, pl.ds(LEAD, width - LEAD)],
            w_ref.at[0, :, pl.ds(LEAD, width - LEAD)],
            load_sems.at[4],
        ),
    ]
    for k in range(1, LINE):
        loads.append(
            pltpu.make_async_copy(
                weight_ref.at[:, pl.ds(k * width, width)], w_ref.at[k], load_sems.at[4 + k]
            )
        )
    for load in loads:
        load.start()

    partners = [device(layer, y, ((me + i) % LINE) // 2, (me + i) % 2) for i in range(1, LINE)]
    partners += [device(layer, (y + i) % NY, z, c) for i in range(1, NY)]
    partners += [device((layer + i) % DEPTH, y, z, c) for i in (1, DEPTH - 1)]
    meet(partners)

    def x_view(slots, core, places):
        rows = slice(places.start * QUARTER, places.stop * QUARTER) if isinstance(places, slice) else (
            pl.ds(places * QUARTER, QUARTER)
        )
        return x_ref.at[slots, core, rows, :]

    activations = Gather(here, x_view, sems[:2])
    factor = Gather(here, lambda slots, core, places: u_ref.at[slots, core, places], sems[2:])

    loads[0].wait()
    mine = panel_ref[...].astype(BF16)
    source = (y == 0) & (z == 0)
    u_ref[0, c, 0] = jnp.where(source, 0.0, panel_ref[...]).astype(BF16)

    def lead_copy(core, target, message):
        return remote(lead_ref.at[core], lead_ref.at[core], lead_send.at[message], lead_recv.at[message], target)

    def lead_z(i):
        return lead_copy(c, device(layer, 0, i, c), i)

    def lead_y(i):
        return lead_copy(c, device(layer, i, z, c), 7 + i)

    def lead_other(core):
        return lead_copy(core, device(layer, y, z, 1 - c), 11)

    @pl.when(source)
    def _():
        lead_ref[c] = mine
        for i in (4, 3, 5, 2, 6, 1, 7):
            lead_z(i).start()

    @pl.when(layer == 0)
    def _():
        loads[1].wait()
        tokens = tokens_ref[...].astype(F32)
        for p in range(LINE):
            for b in range(4):
                at = p * width + b * 128
                pieces_ref[p, PAIR * b : PAIR * (b + 1), :] = tokens[:, at : at + 128]

    by_core(c, lambda core: factor.part(core, 0))

    @pl.when((y == 0) & (z > 0))
    def _():
        lead_copy(c, device(layer, 0, 0, c), z).wait_recv()

    @pl.when(y == 0)
    def _():
        for i in (2, 1, 3):
            lead_y(i).start()

    @pl.when(layer == 0)
    def _():
        wait_tokens = exchange_line(here, pieces_ref, landed_ref, token_send, token_recv)
        wait_tokens()
        for p in range(LINE):
            for b in range(4):
                total_ref[PAIR * p : PAIR * (p + 1), b * 128 : (b + 1) * 128] = landed_ref[
                    p, PAIR * b : PAIR * (b + 1), :
                ]
        x_ref[0, c, :QUARTER, :] = total_ref[:QUARTER, :UNITS].astype(BF16)

    pl.when(layer == 0)(lambda: by_core(c, lambda core: activations.part(core, 0)))

    @pl.when(y > 0)
    def _():
        lead_copy(c, device(layer, 0, z, c), 7 + y).wait_recv()

    lead_other(c).start()
    for load in loads[2:4]:
        load.wait()
    lead_other(1 - c).wait_recv()
    eliminate(leading_ref, mask_ref, lead_ref, pruned_ref, errors_ref, scaled_ref)

    @pl.when(layer > 0)
    def _():
        loads[1].wait()

    for load in loads[4:]:
        load.wait()
    w_ref[0, :, :LEAD] = pruned_ref[...]
    total_ref[...] = jnp.zeros_like(total_ref)
    squares_ref[...] = jnp.zeros_like(squares_ref)

    def factor_and_tokens(core):
        for i in range(1, 5):
            if i < 4:
                activations.part(core, i)
            factor.part(core, i)

    def factor_alone(core):
        for i in range(1, 5):
            factor.part(core, i)

    def hand_on(target):
        return remote(hand_ref, x_ref.at[0, c, pl.ds(0, QUARTER), :], hand_send, hand_recv, target)

    pl.when(layer == 0)(lambda: by_core(c, factor_and_tokens))
    pl.when(layer > 0)(lambda: by_core(c, factor_alone))
    factor.from_other(NEAR, 16)
    factor.from_other(FAR, 17)

    @pl.when(layer > 0)
    def _():
        hand_on(device((layer + DEPTH - 1) % DEPTH, y, z, c)).wait_recv()

        def near_activations(core):
            for i in range(4):
                activations.part(core, i)

        by_core(c, near_activations)

    def multiply(slots, core):
        products, inputs, squares = None, None, None
        for slot in slots:
            k = 2 * slot_z(z, slot) + core
            x = x_ref[slot, core]
            place = y_place(y, k // 4)
            sides = [z_slot(z, 2 * (k % 4)), z_slot(z, 2 * (k % 4) + 1)]
            columns = jnp.concatenate([u_ref[sides[j // 2], j % 2, place] for j in range(4)], 1)
            product = lax.dot_general(x, w_ref[k], TRANSPOSED, preferred_element_type=F32)
            entry = lax.dot_general(x, columns, TRANSPOSED, preferred_element_type=F32)
            wide = x.astype(F32)
            wide = wide * wide
            square = wide[:, :128] + wide[:, 128:256] + wide[:, 256:384] + wide[:, 384:]
            if products is None:
                products, inputs, squares = product, entry, square
            else:
                products, inputs, squares = products + product, inputs + entry, squares + square
        total_ref[:, :UNITS] += products
        total_ref[:, UNITS:] += inputs
        squares_ref[...] += squares

    def both(slots, message):
        numbers = range(slots.start, slots.stop)

        def one(i, carry):
            @pl.when(i == 1)
            def _():
                activations.from_other(slots, message)

            multiply(numbers, c + i * (1 - 2 * c))
            return carry

        lax.fori_loop(0, 2, one, 0)

    both(NEAR, 16)
    by_core(c, lambda core: activations.part(core, 4))
    both(FAR, 17)

    moment = jnp.sum(squares_ref[...], axis=1, keepdims=True) * (UP * UP / FEATURES)
    scale = jnp.where(layer == 0, 1.0, lax.rsqrt(moment + epsilon) * UP)
    inputs = total_ref[:, UNITS:]
    inputs_high = inputs.astype(BF16)
    inputs_low = (inputs - inputs_high.astype(F32)).astype(BF16)
    correction = (
        jnp.dot(inputs_high, errors_ref[0], preferred_element_type=F32)
        + jnp.dot(inputs_low, errors_ref[0], preferred_element_type=F32)
        + jnp.dot(inputs_high, errors_ref[1], preferred_element_type=F32)
    )
    output = ((total_ref[:, :UNITS] - correction) * (scale * FEATURES**-0.5)).astype(BF16)
    for place in range(NY):
        out_ref[place] = output[place * QUARTER : (place + 1) * QUARTER]

    def spread(place):
        dy = {1: 1, 2: NY - 1, 3: 2}[place]
        return remote(
            out_ref.at[place],
            spread_ref.at[BACK[place]],
            spread_send.at[place],
            spread_recv.at[BACK[place]],
            device(layer, (y + dy) % NY, z, c),
        )

    for place in (3, 1, 2):
        spread(place).start()
    residual = x_ref[0, c, :QUARTER, :].astype(F32) * scale[:QUARTER]
    combined = residual + silu(out_ref[0].astype(F32))
    for place in (1, 2, 3):
        spread(BACK[place]).wait_recv()
        combined = combined + silu(spread_ref[place].astype(F32))
    following = device((layer + 1) % DEPTH, y, z, c)

    @pl.when(layer < DEPTH - 1)
    def _():
        hand_ref[...] = (combined * DOWN).astype(BF16)
        hand_on(following).start()

    for p in range(LINE):
        for b in range(4):
            pieces2_ref[p, PAIR * b : PAIR * (b + 1), :] = combined[
                PAIR * p : PAIR * (p + 1), b * 128 : (b + 1) * 128
            ]
    wait_pieces = exchange_line(here, pieces2_ref, landed2_ref, act_send, act_recv)
    wait_pieces()
    pair = landed2_ref[...]
    sums = jnp.sum(jnp.sum(pair * pair, axis=0), axis=1, keepdims=True)
    token = lax.broadcasted_iota(jnp.int32, (PAIR * 4, 1), 0) % PAIR
    mean0 = jnp.sum(jnp.where(token == 0, sums, 0.0), axis=0, keepdims=True) * (1.0 / FEATURES)
    mean1 = jnp.sum(jnp.where(token == 1, sums, 0.0), axis=0, keepdims=True) * (1.0 / FEATURES)
    acts = pair * lax.rsqrt(jnp.where(token == 0, mean0, mean1) + epsilon)[None]
    for p in range(LINE):
        for b in range(4):
            at = p * width + b * 128
            acts_ref[:, at : at + 128] = acts[p, PAIR * b : PAIR * (b + 1), :].astype(BF16)

    by_core(c, factor.finish)
    by_core(c, activations.finish)
    for place in (1, 2, 3):
        spread(place).wait_send()

    @pl.when(source)
    def _():
        for i in range(1, NZ):
            lead_z(i).wait_send()

    @pl.when(y == 0)
    def _():
        for i in range(1, NY):
            lead_y(i).wait_send()

    lead_other(c).wait_send()

    @pl.when(layer < DEPTH - 1)
    def _():
        hand_on(following).wait_send()


def forward(tokens, weight, panel, mask):
    width = FEATURES // LINE
    hbm = pl.BlockSpec(memory_space=pl.ANY)
    vmem = pl.BlockSpec(memory_space=pltpu.VMEM)
    dma = pltpu.SemaphoreType.DMA
    return pl.pallas_call(
        forward_kernel,
        out_shape=(
            jax.ShapeDtypeStruct((PAIR, FEATURES), BF16),
            jax.ShapeDtypeStruct((UNITS, LEAD), BF16),
        ),
        in_specs=[hbm] * 4,
        out_specs=(vmem, vmem),
        scratch_shapes=[
            pltpu.VMEM(tokens.shape, BF16),
            pltpu.VMEM(panel.shape, F32),
            pltpu.VMEM(mask.shape, jnp.int32),
            pltpu.VMEM((UNITS, LEAD), BF16),
            pltpu.VMEM((2, LEAD, BLOCK), BF16),
            pltpu.VMEM((LEAD, UNITS), F32),
            pltpu.VMEM((2, LEAD, UNITS), BF16),
            pltpu.VMEM((Z_SLOTS, 2, TOKENS, width), BF16),
            pltpu.VMEM((LINE, UNITS, width), BF16),
            pltpu.VMEM((Z_SLOTS, 2, Y_PLACES, *panel.shape), BF16),
            pltpu.VMEM((TOKENS, UNITS + LEAD), F32),
            pltpu.VMEM((TOKENS, 128), F32),
            pltpu.VMEM((NY, QUARTER, UNITS), BF16),
            pltpu.VMEM((NY, QUARTER, UNITS), BF16),
            pltpu.VMEM((QUARTER, UNITS), BF16),
            pltpu.VMEM((LINE, PAIR * 4, 128), F32),
            pltpu.VMEM((LINE, PAIR * 4, 128), F32),
            pltpu.VMEM((LINE, PAIR * 4, 128), F32),
            pltpu.VMEM((LINE, PAIR * 4, 128), F32),
            dma((LINE + 4,)),
            dma((12,)),
            dma((12,)),
            dma((LINE,)),
            dma((LINE,)),
            dma((LINE,)),
            dma((LINE,)),
            dma((NY,)),
            dma((NY,)),
            dma,
            dma,
            *GATHER_SEMS,
            *GATHER_SEMS,
        ],
        compiler_params=pltpu.CompilerParams(
            collective_id=0, has_side_effects=True, vmem_limit_bytes=60 * 2**20
        ),
        name="forward",
    )(tokens, weight, panel, mask)


def per_device(tokens, up_weight, hess_panel, keep_mask):
    acts, pruned = forward(tokens, up_weight[0], hess_panel[0], keep_mask[0])
    return (acts[None], pruned[None])


def solution(mesh):
    in_specs = (
        P("row", None),
        P("layer", "row", None),
        P("layer", None, "row"),
        P("layer", "row", None),
    )
    out_specs = (P("layer", "row", None), P("layer", "row", None))
    return jax.shard_map(
        per_device, mesh=mesh, in_specs=in_specs, out_specs=out_specs, check_vma=False
    )
```

time: 203 us -> 140 us (0.69)
  Pallas kernels: 195 us -> 136 us
  local copies, waits for them, and re-layouts: 6.89 us -> 3.07 us
    pallas_call x3 -> x1, Pallas kernels: 195 us -> 136 us  [forward(): pl.pallas_call(forward_kernel, out_shape=(jax.ShapeDtypeStruct((PAIR, FEA...]
    unnamed x11 -> x2, local copies, waits for them, and re-layouts: 6.89 us -> 3.07 us
where the time goes in v1:
time: 140 us
  Pallas kernels  136 us (97%)
  local copies, waits for them, and re-layouts  3.07 us (2%)
    pallas_call x1, Pallas kernels, forward(): pl.pallas_call(forward_kernel, out_shape=(jax.ShapeDtypeStruct((PAIR, FEA...  136 us
    unnamed x2, local copies, waits for them, and re-layouts  3.07 us

profile of v1, /device:TPU:7, one launch (start us, length us, event | category | flops | bytes accessed | tf_op | source)
XLA Modules:
  0.0 139.9 jit_solution(7367401092821685520)
XLA Ops:
  0.6 136.2 %forward.1 = (bf16[2,8192]{1,0:T(2,128)(2,1)}, bf16[512,256]{1,0:T(8,128)(2,1)}) custom-call(bf16[2,8192]{1,0:T(2,128)(2,1)} %tokens_hbm.1, bf16[512,8192]{1,0:T(8,128)(2,1)} %bitcast.5, f32[256,128]{1,0:T(8,128)} %bitcast.8, s32[512,256]{1,0:T(8,128)} %bitcast.6), custom_call_target="tpu_custom_call" | custom-call | tf_op jit(solution)/shard_map/forward/pallas_call | solution.py:610
  136.9 1.4 copy.8
  138.3 1.7 %copy.9 = bf16[1,512,256]{2,1,0:T(8,128)(2,1)} copy(bf16[1,512,256]{2,1,0:T(8,128)(2,1)} %bitcast.7) | data formatting | bytes 524288

commit v2 on v1

--- a/solution.py
+++ b/solution.py
@@ -23,6 +23,7 @@
 TOKENS = 128
 QUARTER = TOKENS // NY
 PAIR = 2
+SHARE = LEAD // NY
 epsilon = 1e-05
 
 DOWN = 2.0**-32
@@ -60,8 +61,6 @@
 Z_SLOTS = 8
 NEAR = slice(0, 5)
 FAR = slice(5, 8)
-Y_PLACES = 4
-BACK = {1: 2, 2: 1, 3: 3}
 
 
 def slot_z(z, k):
@@ -78,11 +77,6 @@
     d = (target - z + NZ) % NZ
     fixed = number(d == 7) + 2 * number(d == 1) + 5 * number(d == 5) + 6 * number(d == 3) + 7 * number(d == 4)
     return fixed + (4 - odd) * number(d == 2) + (3 + odd) * number(d == 6)
-
-
-def y_place(y, target):
-    d = (target - y + NY) % NY
-    return d + number(d == 2) - number(d == 3)
 
 
 class Gather:
@@ -96,16 +90,16 @@
         self.behind_in, self.ahead_in = 2 + odd, 3 - odd
         self.behind_slot, self.behind_out = 5 + odd, 4 + odd
         self.ahead_slot, self.ahead_out = 6 - odd, 5 - odd
-        self.sent = {0: {}, 1: {}}
+        self.sent = {}
 
     def copy(self, core, src, dst, dy, dz, message):
-        src, dst = (self.view(slots, core, places) for slots, places in (src, dst))
+        src, dst = (self.view(slots, core, part) for slots, part in (src, dst))
         target = device(self.layer, (self.y + dy + NY) % NY, (self.z + dz + NZ) % NZ, core)
         return remote(src, dst, self.send_sems.at[message], self.recv_sems.at[message], target)
 
     def send(self, core, src, dst, dy, dz, message, name=None):
         self.copy(core, src, dst, dy, dz, message).start()
-        self.sent[core][name or message] = lambda: self.copy(core, src, dst, dy, dz, message).wait_send()
+        self.keep(core, name or message, lambda core: self.copy(core, src, dst, dy, dz, message).wait_send())
 
     def arrive(self, core, dst, message):
         self.copy(core, dst, dst, 1, 0, message).wait_recv()
@@ -129,39 +123,48 @@
         for slot in slots:
             self.arrive(core, (slot, places), {1: 0, 2: 1, 5: 4, 6: 5, 7: 6}[slot])
 
-    def y_out(self, core, slots, message):
-        own = (slots, 0)
-        for place, dy in ((3, 2), (1, 1), (2, -1)):
-            self.send(core, own, (slots, BACK[place]), dy, 0, message + place - 1)
-
-    def y_in(self, core, slots, message):
-        for place in (1, 2, 3):
-            self.arrive(core, (slots, place), message + BACK[place] - 1)
-
     def other(self, core, slots, message):
-        view = self.view(slots, core, slice(0, Y_PLACES))
-        target = device(self.layer, self.y, self.z, 1 - self.c)
+        view = self.view(slots, core, None)
+        target = device(self.layer, self.y, self.z, 1 - core)
         return remote(view, view, self.send_sems.at[message], self.recv_sems.at[message], target)
 
     def to_other(self, core, slots, message):
         self.other(core, slots, message).start()
-        self.sent[core][message] = lambda: self.other(core, slots, message).wait_send()
+        self.keep(core, message, lambda core: self.other(core, slots, message).wait_send())
 
     def from_other(self, slots, message):
         self.other(1 - self.c, slots, message).wait_recv()
 
+    def keep(self, core, name, wait):
+        branch = core if isinstance(core, int) else "both"
+        self.sent.setdefault(branch, {})[name] = wait
+
+    def finish(self, core):
+        for wait in self.sent[core if isinstance(core, int) else "both"].values():
+            wait(core)
+
+
+class TokenGather(Gather):
+    def y_out(self, core, slots, message):
+        own = (slots, self.y)
+        for dy in (2, 1, 3):
+            self.send(core, own, own, dy, 0, message + dy - 1)
+
+    def y_in(self, core, slots, message):
+        for dy in (1, 3, 2):
+            self.arrive(core, (slots, (self.y + NY - dy) % NY), message + dy - 1)
+
     def part(self, core, i):
-        every = slice(0, Y_PLACES)
         if core == 0:
             if i == 0:
-                self.z_out(core, 0)
+                self.z_out(core, self.y)
                 self.y_out(core, 0, 7)
             elif i == 1:
-                self.z_relay(core, 0)
-                self.z_in(core, 0, (1, 2))
+                self.z_relay(core, self.y)
+                self.z_in(core, self.y, (1, 2))
                 self.y_out(core, slice(1, 5), 10)
             elif i == 2:
-                self.z_in(core, 0, (5, 6, 7))
+                self.z_in(core, self.y, (5, 6, 7))
                 self.y_out(core, FAR, 13)
             elif i == 3:
                 self.y_in(core, 0, 7)
@@ -175,19 +178,49 @@
                 self.y_out(core, 0, 7)
             elif i == 1:
                 self.y_in(core, 0, 7)
-                self.z_out(core, every)
+                self.z_out(core, None)
             elif i == 2:
-                self.z_relay(core, every)
+                self.z_relay(core, None)
             elif i == 3:
-                self.z_in(core, every, (1, 2))
+                self.z_in(core, None, (1, 2))
                 self.to_other(core, NEAR, 16)
             else:
-                self.z_in(core, every, (5, 6, 7))
+                self.z_in(core, None, (5, 6, 7))
                 self.to_other(core, FAR, 17)
 
-    def finish(self, core):
-        for wait in self.sent[core].values():
-            wait()
+
+class FactorGather(Gather):
+    def __init__(self, here, own_ref, landing, view, sems):
+        super().__init__(here, view, sems)
+        self.own_ref, self.landing = own_ref, landing
+
+    def rows_to(self, dy):
+        to = (self.y + dy) % NY
+        return remote(
+            self.own_ref.at[pl.ds(to * SHARE, SHARE)],
+            self.landing(to),
+            self.send_sems.at[6 + dy],
+            self.recv_sems.at[6 + dy],
+            device(self.layer, to, self.z, self.c),
+        )
+
+    def part(self, core, i):
+        if i == 0:
+            for dy in (2, 1, 3):
+                self.rows_to(dy).start()
+                self.keep(core, 6 + dy, lambda core, dy=dy: self.rows_to(dy).wait_send())
+        elif i == 1:
+            for dy in (1, 3, 2):
+                self.arrive(core, (0, (self.y + NY - dy) % NY), 6 + dy)
+            self.z_out(core, None)
+        elif i == 2:
+            self.z_relay(core, None)
+        elif i == 3:
+            self.z_in(core, None, (1, 2))
+            self.to_other(core, NEAR, 16)
+        else:
+            self.z_in(core, None, (5, 6, 7))
+            self.to_other(core, FAR, 17)
 
 
 GATHER_SEMS = [pltpu.SemaphoreType.DMA((18,)), pltpu.SemaphoreType.DMA((18,))]
@@ -265,39 +298,23 @@
     errors_ref[1] = jnp.concatenate(low, 0)
 
 
-def exchange_line(here, pieces, landed, send_sems, recv_sems):
+def exchange_line(here, pieces, landed, send_sem, recv_sem):
     layer, y, z, c = here
     me = 2 * z + c
-
-    def message(i):
+    for i in range(1, LINE):
         peer = (me + i) % LINE
-        return remote(
-            pieces.at[peer],
-            landed.at[me],
-            send_sems.at[i],
-            recv_sems.at[i],
-            device(layer, y, peer // 2, peer % 2),
-        )
-
-    def start(i, carry):
-        message(i).start()
-        return carry
-
-    def wait(i, carry):
-        source = (me + LINE - i) % LINE
         remote(
-            pieces.at[source],
-            landed.at[source],
-            send_sems.at[i],
-            recv_sems.at[i],
-            device(layer, y, source // 2, source % 2),
-        ).wait_recv()
-        message(i).wait_send()
-        return carry
-
-    lax.fori_loop(1, LINE, start, 0)
+            pieces.at[peer], landed.at[me], send_sem, recv_sem, device(layer, y, peer // 2, peer % 2)
+        ).start()
     landed[me] = pieces[me]
-    return lambda: lax.fori_loop(1, LINE, wait, 0)
+
+
+def exchange_wait(here, pieces, landed, send_sem, recv_sem):
+    layer, y, z, c = here
+    others = pl.ds(0, LINE - 1)
+    every = remote(pieces.at[others], landed.at[others], send_sem, recv_sem, device(layer, y, z, 1 - c))
+    every.wait_recv()
+    every.wait_send()
 
 
 def silu(v):
@@ -322,7 +339,11 @@
     w_ref,
     u_ref,
     total_ref,
+    inputs_ref,
+    every_input_ref,
+    own_ref,
     squares_ref,
+    scale_ref,
     out_ref,
     spread_ref,
     hand_ref,
@@ -337,6 +358,10 @@
     token_recv,
     act_send,
     act_recv,
+    share_send,
+    share_recv,
+    inputs_send,
+    inputs_recv,
     spread_send,
     spread_recv,
     hand_send,
@@ -373,19 +398,22 @@
     partners += [device((layer + i) % DEPTH, y, z, c) for i in (1, DEPTH - 1)]
     meet(partners)
 
-    def x_view(slots, core, places):
-        rows = slice(places.start * QUARTER, places.stop * QUARTER) if isinstance(places, slice) else (
-            pl.ds(places * QUARTER, QUARTER)
-        )
+    def x_view(slots, core, part):
+        rows = pl.ds(0, TOKENS) if part is None else pl.ds(pl.multiple_of(part * QUARTER, QUARTER), QUARTER)
         return x_ref.at[slots, core, rows, :]
 
-    activations = Gather(here, x_view, sems[:2])
-    factor = Gather(here, lambda slots, core, places: u_ref.at[slots, core, places], sems[2:])
+    def u_view(slots, core, part):
+        return u_ref.at[y, slots, core] if part is None else u_ref.at[y, slots, core, part]
+
+    activations = TokenGather(here, x_view, sems[:2])
+    factor = FactorGather(here, own_ref, lambda to: u_ref.at[to, 0, c, y], u_view, sems[2:])
 
     loads[0].wait()
     mine = panel_ref[...].astype(BF16)
     source = (y == 0) & (z == 0)
-    u_ref[0, c, 0] = jnp.where(source, 0.0, panel_ref[...]).astype(BF16)
+    my_rows = pl.ds(pl.multiple_of(y * QUARTER, QUARTER), QUARTER)
+    own_ref[...] = jnp.where(source, 0.0, panel_ref[...]).astype(BF16)
+    u_ref[y, 0, c, y] = own_ref[pl.ds(pl.multiple_of(y * SHARE, SHARE), SHARE), :]
 
     def lead_copy(core, target, message):
         return remote(lead_ref.at[core], lead_ref.at[core], lead_send.at[message], lead_recv.at[message], target)
@@ -413,8 +441,9 @@
             for b in range(4):
                 at = p * width + b * 128
                 pieces_ref[p, PAIR * b : PAIR * (b + 1), :] = tokens[:, at : at + 128]
-
-    by_core(c, lambda core: factor.part(core, 0))
+        exchange_line(here, pieces_ref, landed_ref, token_send, token_recv)
+
+    factor.part(c, 0)
 
     @pl.when((y == 0) & (z > 0))
     def _():
@@ -427,22 +456,47 @@
 
     @pl.when(layer == 0)
     def _():
-        wait_tokens = exchange_line(here, pieces_ref, landed_ref, token_send, token_recv)
-        wait_tokens()
+        exchange_wait(here, pieces_ref, landed_ref, token_send, token_recv)
         for p in range(LINE):
             for b in range(4):
                 total_ref[PAIR * p : PAIR * (p + 1), b * 128 : (b + 1) * 128] = landed_ref[
                     p, PAIR * b : PAIR * (b + 1), :
                 ]
-        x_ref[0, c, :QUARTER, :] = total_ref[:QUARTER, :UNITS].astype(BF16)
-
-    pl.when(layer == 0)(lambda: by_core(c, lambda core: activations.part(core, 0)))
+        x_ref[0, c, my_rows, :] = total_ref[:QUARTER, :].astype(BF16)
+
+    def gather_parts(*parts):
+        for i in parts:
+            pl.when(layer == 0)(lambda: by_core(c, lambda core: activations.part(core, i)))
+            if i:
+                factor.part(c, i)
+
+    gather_parts(0, 1, 2)
 
     @pl.when(y > 0)
     def _():
         lead_copy(c, device(layer, 0, z, c), 7 + y).wait_recv()
 
     lead_other(c).start()
+    gather_parts(3)
+
+    def share_to(dy):
+        mine = u_ref.at[y, :, c]
+        return remote(mine, mine, share_send.at[dy], share_recv.at[dy], device(layer, (y + dy) % NY, z, c))
+
+    def share_from(dy, core):
+        theirs = u_ref.at[(y + NY - dy) % NY, :, core]
+        return remote(
+            theirs, theirs, share_send.at[3 + dy], share_recv.at[3 + dy], device(layer, y, z, 1 - c)
+        )
+
+    @pl.when(layer > 0)
+    def _():
+        factor.part(c, 4)
+        factor.from_other(NEAR, 16)
+        factor.from_other(FAR, 17)
+        for dy in (2, 1, 3):
+            share_to(dy).start()
+
     for load in loads[2:4]:
         load.wait()
     lead_other(1 - c).wait_recv()
@@ -456,28 +510,34 @@
         load.wait()
     w_ref[0, :, :LEAD] = pruned_ref[...]
     total_ref[...] = jnp.zeros_like(total_ref)
+    inputs_ref[y] = jnp.zeros_like(inputs_ref[y])
+    every_input_ref[...] = jnp.zeros_like(every_input_ref)
     squares_ref[...] = jnp.zeros_like(squares_ref)
 
-    def factor_and_tokens(core):
-        for i in range(1, 5):
-            if i < 4:
-                activations.part(core, i)
-            factor.part(core, i)
-
-    def factor_alone(core):
-        for i in range(1, 5):
-            factor.part(core, i)
+    @pl.when(layer == 0)
+    def _():
+        factor.part(c, 4)
+        factor.from_other(NEAR, 16)
+        factor.from_other(FAR, 17)
 
     def hand_on(target):
-        return remote(hand_ref, x_ref.at[0, c, pl.ds(0, QUARTER), :], hand_send, hand_recv, target)
-
-    pl.when(layer == 0)(lambda: by_core(c, factor_and_tokens))
-    pl.when(layer > 0)(lambda: by_core(c, factor_alone))
-    factor.from_other(NEAR, 16)
-    factor.from_other(FAR, 17)
+        return remote(hand_ref, x_ref.at[0, c, my_rows, :], hand_send, hand_recv, target)
+
+    def inputs_to(dy):
+        mine = inputs_ref.at[y]
+        return remote(mine, mine, inputs_send.at[dy], inputs_recv.at[dy], device(layer, (y + dy) % NY, z, c))
 
     @pl.when(layer > 0)
     def _():
+        for dy in (1, 3, 2):
+            theirs = u_ref.at[(y + NY - dy) % NY, :, c]
+            target = device(layer, (y + dy) % NY, z, c)
+            remote(theirs, theirs, share_send.at[dy], share_recv.at[dy], target).wait_recv()
+            share_from(dy, c).start()
+        for dy in (1, 3, 2):
+            share_from(dy, 1 - c).wait_recv()
+            share_from(dy, c).wait_send()
+            share_to(dy).wait_send()
         hand_on(device((layer + DEPTH - 1) % DEPTH, y, z, c)).wait_recv()
 
         def near_activations(core):
@@ -486,47 +546,81 @@
 
         by_core(c, near_activations)
 
-    def multiply(slots, core):
-        products, inputs, squares = None, None, None
+    def add(old, new):
+        return new if old is None else old + new
+
+    def multiply(slots, core, shares=(), weights=True, turned=False):
+        products, entries, squares = None, None, None
         for slot in slots:
             k = 2 * slot_z(z, slot) + core
             x = x_ref[slot, core]
-            place = y_place(y, k // 4)
-            sides = [z_slot(z, 2 * (k % 4)), z_slot(z, 2 * (k % 4) + 1)]
-            columns = jnp.concatenate([u_ref[sides[j // 2], j % 2, place] for j in range(4)], 1)
-            product = lax.dot_general(x, w_ref[k], TRANSPOSED, preferred_element_type=F32)
-            entry = lax.dot_general(x, columns, TRANSPOSED, preferred_element_type=F32)
-            wide = x.astype(F32)
-            wide = wide * wide
-            square = wide[:, :128] + wide[:, 128:256] + wide[:, 256:384] + wide[:, 384:]
-            if products is None:
-                products, inputs, squares = product, entry, square
+            if weights:
+                products = add(
+                    products, lax.dot_general(x, w_ref[k], TRANSPOSED, preferred_element_type=F32)
+                )
+            if shares:
+                sides = [z_slot(z, 2 * (k % 4)), z_slot(z, 2 * (k % 4) + 1)]
+                columns = [
+                    jnp.concatenate([u_ref[share, sides[j // 2], j % 2, k // 4] for j in range(4)], 1)
+                    for share in shares
+                ]
+                columns = columns[0] if len(columns) == 1 else jnp.concatenate(columns, 0)
+                left, right = (columns, x) if turned else (x, columns)
+                entries = add(entries, lax.dot_general(left, right, TRANSPOSED, preferred_element_type=F32))
+                wide = x.astype(F32)
+                wide = wide * wide
+                squares = add(
+                    squares, wide[:, :128] + wide[:, 128:256] + wide[:, 256:384] + wide[:, 384:]
+                )
+        if weights:
+            total_ref[...] += products
+        if shares:
+            if turned:
+                inputs_ref[y] += entries
             else:
-                products, inputs, squares = products + product, inputs + entry, squares + square
-        total_ref[:, :UNITS] += products
-        total_ref[:, UNITS:] += inputs
-        squares_ref[...] += squares
-
-    def both(slots, message):
-        numbers = range(slots.start, slots.stop)
-
+                every_input_ref[...] += entries
+            squares_ref[...] += squares
+
+    def both(numbers, message, **what):
         def one(i, carry):
-            @pl.when(i == 1)
-            def _():
-                activations.from_other(slots, message)
-
-            multiply(numbers, c + i * (1 - 2 * c))
+            if message is not None:
+
+                @pl.when(i == 1)
+                def _():
+                    activations.from_other(slice(numbers.start, numbers.stop), message)
+
+            multiply(numbers, c + i * (1 - 2 * c), **what)
             return carry
 
         lax.fori_loop(0, 2, one, 0)
 
-    both(NEAR, 16)
-    by_core(c, lambda core: activations.part(core, 4))
-    both(FAR, 17)
+    near, far = range(NEAR.start, NEAR.stop), range(FAR.start, FAR.stop)
+
+    @pl.when(layer == 0)
+    def _():
+        both(near, 16, shares=[y], turned=True)
+        by_core(c, lambda core: activations.part(core, 4))
+        both(far, 17, shares=[y], weights=False, turned=True)
+        for dy in (2, 1, 3):
+            inputs_to(dy).start()
+        both(far, None)
+        for dy in (1, 3, 2):
+            theirs = inputs_ref.at[(y + NY - dy) % NY]
+            target = device(layer, (y + dy) % NY, z, c)
+            remote(theirs, theirs, inputs_send.at[dy], inputs_recv.at[dy], target).wait_recv()
+        for dy in (1, 3, 2):
+            inputs_to(dy).wait_send()
+        every_input_ref[...] = jnp.concatenate([inputs_ref[i] for i in range(NY)], 0).T
+
+    @pl.when(layer > 0)
+    def _():
+        both(near, 16, shares=list(range(NY)))
+        by_core(c, lambda core: activations.part(core, 4))
+        both(far, 17, shares=list(range(NY)))
 
     moment = jnp.sum(squares_ref[...], axis=1, keepdims=True) * (UP * UP / FEATURES)
     scale = jnp.where(layer == 0, 1.0, lax.rsqrt(moment + epsilon) * UP)
-    inputs = total_ref[:, UNITS:]
+    inputs = every_input_ref[...]
     inputs_high = inputs.astype(BF16)
     inputs_low = (inputs - inputs_high.astype(F32)).astype(BF16)
     correction = (
@@ -534,27 +628,24 @@
         + jnp.dot(inputs_low, errors_ref[0], preferred_element_type=F32)
         + jnp.dot(inputs_high, errors_ref[1], preferred_element_type=F32)
     )
-    output = ((total_ref[:, :UNITS] - correction) * (scale * FEATURES**-0.5)).astype(BF16)
-    for place in range(NY):
-        out_ref[place] = output[place * QUARTER : (place + 1) * QUARTER]
-
-    def spread(place):
-        dy = {1: 1, 2: NY - 1, 3: 2}[place]
+    output = ((total_ref[...] - correction) * (scale * FEATURES**-0.5)).astype(BF16)
+    for q in range(NY):
+        out_ref[q] = output[q * QUARTER : (q + 1) * QUARTER]
+    scale_ref[...] = jnp.broadcast_to(scale, scale_ref.shape)
+
+    def spread(dy):
+        q = (y + dy) % NY
         return remote(
-            out_ref.at[place],
-            spread_ref.at[BACK[place]],
-            spread_send.at[place],
-            spread_recv.at[BACK[place]],
-            device(layer, (y + dy) % NY, z, c),
+            out_ref.at[q], spread_ref.at[dy], spread_send.at[dy], spread_recv.at[dy], device(layer, q, z, c)
         )
 
-    for place in (3, 1, 2):
-        spread(place).start()
-    residual = x_ref[0, c, :QUARTER, :].astype(F32) * scale[:QUARTER]
-    combined = residual + silu(out_ref[0].astype(F32))
-    for place in (1, 2, 3):
-        spread(BACK[place]).wait_recv()
-        combined = combined + silu(spread_ref[place].astype(F32))
+    for dy in (2, 1, 3):
+        spread(dy).start()
+    residual = x_ref[0, c, my_rows, :].astype(F32) * scale_ref[my_rows, :1]
+    combined = residual + silu(out_ref[y].astype(F32))
+    for dy in (1, 3, 2):
+        spread(dy).wait_recv()
+        combined = combined + silu(spread_ref[dy].astype(F32))
     following = device((layer + 1) % DEPTH, y, z, c)
 
     @pl.when(layer < DEPTH - 1)
@@ -567,8 +658,28 @@
             pieces2_ref[p, PAIR * b : PAIR * (b + 1), :] = combined[
                 PAIR * p : PAIR * (p + 1), b * 128 : (b + 1) * 128
             ]
-    wait_pieces = exchange_line(here, pieces2_ref, landed2_ref, act_send, act_recv)
-    wait_pieces()
+    exchange_line(here, pieces2_ref, landed2_ref, act_send, act_recv)
+    factor.finish(c)
+    by_core(c, activations.finish)
+    for dy in (1, 2, 3):
+        spread(dy).wait_send()
+
+    @pl.when(source)
+    def _():
+        for i in range(1, NZ):
+            lead_z(i).wait_send()
+
+    @pl.when(y == 0)
+    def _():
+        for i in range(1, NY):
+            lead_y(i).wait_send()
+
+    lead_other(c).wait_send()
+
+    @pl.when(layer < DEPTH - 1)
+    def _():
+        hand_on(following).wait_send()
+    exchange_wait(here, pieces2_ref, landed2_ref, act_send, act_recv)
     pair = landed2_ref[...]
     sums = jnp.sum(jnp.sum(pair * pair, axis=0), axis=1, keepdims=True)
     token = lax.broadcasted_iota(jnp.int32, (PAIR * 4, 1), 0) % PAIR
@@ -579,27 +690,6 @@
         for b in range(4):
             at = p * width + b * 128
             acts_ref[:, at : at + 128] = acts[p, PAIR * b : PAIR * (b + 1), :].astype(BF16)
-
-    by_core(c, factor.finish)
-    by_core(c, activations.finish)
-    for place in (1, 2, 3):
-        spread(place).wait_send()
-
-    @pl.when(source)
-    def _():
-        for i in range(1, NZ):
-            lead_z(i).wait_send()
-
-    @pl.when(y == 0)
-    def _():
-        for i in range(1, NY):
-            lead_y(i).wait_send()
-
-    lead_other(c).wait_send()
-
-    @pl.when(layer < DEPTH - 1)
-    def _():
-        hand_on(following).wait_send()
 
 
 def forward(tokens, weight, panel, mask):
@@ -625,8 +715,12 @@
             pltpu.VMEM((2, LEAD, UNITS), BF16),
             pltpu.VMEM((Z_SLOTS, 2, TOKENS, width), BF16),
             pltpu.VMEM((LINE, UNITS, width), BF16),
-            pltpu.VMEM((Z_SLOTS, 2, Y_PLACES, *panel.shape), BF16),
-            pltpu.VMEM((TOKENS, UNITS + LEAD), F32),
+            pltpu.VMEM((NY, Z_SLOTS, 2, NY, SHARE, 128), BF16),
+            pltpu.VMEM((TOKENS, UNITS), F32),
+            pltpu.VMEM((NY, SHARE, TOKENS), F32),
+            pltpu.VMEM((TOKENS, LEAD), F32),
+            pltpu.VMEM(panel.shape, BF16),
+            pltpu.VMEM((TOKENS, 128), F32),
             pltpu.VMEM((TOKENS, 128), F32),
             pltpu.VMEM((NY, QUARTER, UNITS), BF16),
             pltpu.VMEM((NY, QUARTER, UNITS), BF16),
@@ -638,10 +732,14 @@
             dma((LINE + 4,)),
             dma((12,)),
             dma((12,)),
-            dma((LINE,)),
-            dma((LINE,)),
-            dma((LINE,)),
-            dma((LINE,)),
+            dma,
+            dma,
+            dma,
+            dma,
+            dma((7,)),
+            dma((7,)),
+            dma((NY,)),
+            dma((NY,)),
             dma((NY,)),
             dma((NY,)),
             dma,
@@ -656,8 +754,27 @@
     )(tokens, weight, panel, mask)
 
 
+def hand_out_kernel(acts_in, pruned_in, acts_out, pruned_out):
+    acts_out[...] = acts_in[...]
+    pruned_out[...] = pruned_in[...]
+
+
+def hand_out(acts, pruned):
+    vmem = pl.BlockSpec(memory_space=pltpu.VMEM)
+    return pl.pallas_call(
+        hand_out_kernel,
+        out_shape=(
+            jax.ShapeDtypeStruct(acts.shape, acts.dtype),
+            jax.ShapeDtypeStruct(pruned.shape, pruned.dtype),
+        ),
+        in_specs=[vmem, vmem],
+        out_specs=(vmem, vmem),
+        name="hand_out",
+    )(acts, pruned)
+
+
 def per_device(tokens, up_weight, hess_panel, keep_mask):
-    acts, pruned = forward(tokens, up_weight[0], hess_panel[0], keep_mask[0])
+    acts, pruned = hand_out(*forward(tokens, up_weight[0], hess_panel[0], keep_mask[0]))
     return (acts[None], pruned[None])
 
 

time: 140 us -> 129 us (0.921)
  Pallas kernels: 136 us -> 128 us
  local copies, waits for them, and re-layouts: 3.07 us -> 0 us
    pallas_call x1, Pallas kernels: 136 us -> 126 us  [forward(): pl.pallas_call(forward_kernel, out_shape=(jax.ShapeDtypeStruct((PAIR, FEA...]
    unnamed x2 -> x0, local copies, waits for them, and re-layouts: 3.07 us -> none
    pallas_call x0 -> x1, Pallas kernels: none -> 1.69 us  [hand_out(): pl.pallas_call(hand_out_kernel, out_shape=(jax.ShapeDtypeStruct(acts.shap...]
where the time goes in v2:
time: 129 us
  Pallas kernels  128 us (99%)
    pallas_call x1, Pallas kernels, forward(): pl.pallas_call(forward_kernel, out_shape=(jax.ShapeDtypeStruct((PAIR, FEA...  126 us

profile of v2, /device:TPU:7, one launch (start us, length us, event | category | flops | bytes accessed | tf_op | source)
XLA Modules:
  0.0 128.8 jit_solution(7044151126231980635)
XLA Ops:
  0.6 126.5 %forward.1 = (bf16[2,8192]{1,0:T(2,128)(2,1)}, bf16[512,256]{1,0:T(8,128)(2,1)}) custom-call(bf16[2,8192]{1,0:T(2,128)(2,1)} %tokens_hbm.1, bf16[512,8192]{1,0:T(8,128)(2,1)} %bitcast.5, f32[256,128]{1,0:T(8,128)} %bitcast.7, s32[512,256]{1,0:T(8,128)} %bitcast.6), custom_call_target="tpu_custom_call" | custom-call | tf_op jit(solution)/shard_map/forward/pallas_call | solution.py:700
  127.1 1.7 %hand_out.1 = (bf16[2,8192]{1,0:T(2,128)(2,1)}, bf16[512,256]{1,0:T(8,128)(2,1)}) custom-call(bf16[2,8192]{1,0:T(2,128)(2,1)} %get-tuple-element.6.acts_in, bf16[512,256]{1,0:T(8,128)(2,1)} %get-tuple-element.7.pruned_in), custom_call_target="tpu_custom_call" | custom-call | tf_op jit(solution)/shard_map/hand_out/pallas_call | solution.py:764

commit v3 on v2

--- a/solution.py
+++ b/solution.py
@@ -581,12 +581,14 @@
                 every_input_ref[...] += entries
             squares_ref[...] += squares
 
-    def both(numbers, message, **what):
+    def both(numbers, message, between=None, **what):
         def one(i, carry):
             if message is not None:
 
                 @pl.when(i == 1)
                 def _():
+                    if between is not None:
+                        between()
                     activations.from_other(slice(numbers.start, numbers.stop), message)
 
             multiply(numbers, c + i * (1 - 2 * c), **what)
@@ -614,8 +616,8 @@
 
     @pl.when(layer > 0)
     def _():
-        both(near, 16, shares=list(range(NY)))
-        by_core(c, lambda core: activations.part(core, 4))
+        hand_far = lambda: by_core(c, lambda core: activations.part(core, 4))
+        both(near, 16, between=hand_far, shares=list(range(NY)))
         both(far, 17, shares=list(range(NY)))
 
     moment = jnp.sum(squares_ref[...], axis=1, keepdims=True) * (UP * UP / FEATURES)

time: 129 us -> 132 us (1.023)
  Pallas kernels: 128 us -> 131 us
    pallas_call x1, Pallas kernels: 126 us -> 130 us  [forward(): pl.pallas_call(forward_kernel, out_shape=(jax.ShapeDtypeStruct((PAIR, FEA...]
where the time goes in v3:
time: 132 us
  Pallas kernels  131 us (99%)
    pallas_call x1, Pallas kernels, forward(): pl.pallas_call(forward_kernel, out_shape=(jax.ShapeDtypeStruct((PAIR, FEA...  130 us

profile of v3, /device:TPU:7, one launch (start us, length us, event | category | flops | bytes accessed | tf_op | source)
XLA Modules:
  0.0 132.0 jit_solution(1186796430768580460)
XLA Ops:
  0.6 129.7 %forward.1 = (bf16[2,8192]{1,0:T(2,128)(2,1)}, bf16[512,256]{1,0:T(8,128)(2,1)}) custom-call(bf16[2,8192]{1,0:T(2,128)(2,1)} %tokens_hbm.1, bf16[512,8192]{1,0:T(8,128)(2,1)} %bitcast.5, f32[256,128]{1,0:T(8,128)} %bitcast.7, s32[512,256]{1,0:T(8,128)} %bitcast.6), custom_call_target="tpu_custom_call" | custom-call | tf_op jit(solution)/shard_map/forward/pallas_call | solution.py:702
  130.3 1.7 %hand_out.1 = (bf16[2,8192]{1,0:T(2,128)(2,1)}, bf16[512,256]{1,0:T(8,128)(2,1)}) custom-call(bf16[2,8192]{1,0:T(2,128)(2,1)} %get-tuple-element.6.acts_in, bf16[512,256]{1,0:T(8,128)(2,1)} %get-tuple-element.7.pruned_in), custom_call_target="tpu_custom_call" | custom-call | tf_op jit(solution)/shard_map/hand_out/pallas_call | solution.py:766
